TPU v7x, 32 devices: a whole 2x2x4 slice. The times are simulated.
32 devices in a mesh: dp: 8 (over y, x, core), seq: 4 (over z).
Axes of the slice: x: 2, y: 2, z: 4, core: 2. Of those that a mesh axis runs over, the one named last changes fastest.
Arguments:
- inputs: bfloat16 [32768, 768], P(('dp', 'seq')), may hold values from -6 to 6
- attn_gain: bfloat16 [768], P('dp'), may hold values from 0.25 to 1.75
- qkv_weight: bfloat16 [768, 2304], P('dp'), may hold values from -0.25 to 0.25
- proj_weight: bfloat16 [768, 768], P('dp'), may hold values from -0.4375 to 0.4375
- mlp_gain: bfloat16 [768], P('dp'), may hold values from 0.25 to 1.75
- in_weight: bfloat16 [768, 2304], P('dp'), may hold values from -0.21875 to 0.21875
- out_weight: bfloat16 [1152, 768], P('dp'), may hold values from -0.25 to 0.25
- cotangent: bfloat16 [32768, 768], P(('dp', 'seq')), may hold values from -12 to 12
Outputs:
- output: bfloat16 [32768, 768], P(('dp', 'seq'))
- input_grad: bfloat16 [32768, 768], P(('dp', 'seq'))
- attn_gain_grad: float32 [768], P('dp')
- qkv_weight_grad: float32 [768, 2304], P('dp')
- proj_weight_grad: float32 [768, 768], P('dp')
- mlp_gain_grad: float32 [768], P('dp')
- in_weight_grad: float32 [768, 2304], P('dp')
- out_weight_grad: float32 [1152, 768], P('dp')
All inputs are finite; a program needn't handle non-finite values.
Results may differ from a plain program's by a relative error of at most 0.02.
Values may be sent and summed in bfloat16 or wider, within the bound.
A program may use at most 128 MiB of HBM per device.

v0:
```python
import jax
import jax.numpy as jnp
from jax import lax
from jax.sharding import PartitionSpec as P

D = 768
HEADS = 12
HEAD_DIM = 64
FF = 1152
WINDOW = 64
QBLOCK = 512
epsilon = 1e-05
theta_base = 10000.0
masked_score = -1e30


def layer_norm(features, gain_vector):
    center = features - jnp.mean(features, -1, keepdims=True)
    spread = jnp.mean(center * center, -1, keepdims=True)
    return center * lax.rsqrt(spread + epsilon) * gain_vector


def rotary_tables(positions, head_width):
    half_width = head_width // 2
    inverse_freq = theta_base ** (-(jnp.arange(half_width, dtype=jnp.float32) * 2.0) / head_width)
    angles = positions[:, None] * inverse_freq[None, :]
    cosine_table = jnp.concatenate([jnp.cos(angles), jnp.cos(angles)], -1)
    sine_table = jnp.concatenate([jnp.sin(angles), jnp.sin(angles)], -1)
    return (cosine_table[:, None, :], sine_table[:, None, :])


def rotate(features, cosine_table, sine_table):
    half_width = features.shape[-1] // 2
    turned = jnp.concatenate([-features[..., half_width:], features[..., :half_width]], -1)
    return features * cosine_table + turned * sine_table


def gated_gelu(up_values):
    gelu_input = up_values[:, :FF]
    gate_half = up_values[:, FF:]
    return jax.nn.gelu(gelu_input, approximate=False) * gate_half


def band_scores(query_block, key_block, first_row, seq_total):
    score_scale = query_block.shape[-1] ** (-0.5)
    key_span = key_block.shape[0]
    scores = (
        jnp.einsum("qhd,khd->hqk", query_block, key_block, preferred_element_type=jnp.float32)
        * score_scale
    )
    query_pos = first_row + jnp.arange(QBLOCK, dtype=jnp.int32)[:, None]
    key_pos = first_row - WINDOW + jnp.arange(key_span, dtype=jnp.int32)[None, :]
    in_band = (jnp.abs(query_pos - key_pos) <= WINDOW) & (key_pos >= 0) & (key_pos < seq_total)
    return jnp.where(in_band[None], scores, masked_score)


def band_forward(queries, key_pad, value_pad, offset, seq_total):
    row_count = queries.shape[0]
    key_span = QBLOCK + 2 * WINDOW

    def one_block(block_index):
        row_start = block_index * QBLOCK
        query_block = lax.dynamic_slice_in_dim(queries, row_start, QBLOCK, 0)
        key_block = lax.dynamic_slice_in_dim(key_pad, row_start, key_span, 0)
        value_block = lax.dynamic_slice_in_dim(value_pad, row_start, key_span, 0)
        scores = band_scores(query_block, key_block, offset + row_start, seq_total)
        row_max = jnp.max(scores, -1, keepdims=True)
        weights = jnp.exp(scores - row_max)
        row_sum = jnp.sum(weights, -1, keepdims=True)
        softmax_low = (weights / row_sum).astype(jnp.bfloat16)
        result = jnp.einsum(
            "hqk,khd->qhd", softmax_low, value_block, preferred_element_type=jnp.float32
        )
        log_sum = jnp.transpose((row_max + jnp.log(row_sum))[:, :, 0])
        return (result, log_sum)

    results, log_sums = lax.map(one_block, jnp.arange(row_count // QBLOCK, dtype=jnp.int32))
    return (results.reshape(queries.shape), log_sums.reshape(row_count, queries.shape[1]))


def band_backward(queries, key_pad, value_pad, grad_out, log_sums, offset, seq_total):
    row_count = queries.shape[0]
    key_span = QBLOCK + 2 * WINDOW
    score_scale = queries.shape[-1] ** (-0.5)

    def one_block(carried, block_index):
        key_grads, value_grads = carried
        row_start = block_index * QBLOCK
        query_block = lax.dynamic_slice_in_dim(queries, row_start, QBLOCK, 0)
        key_block = lax.dynamic_slice_in_dim(key_pad, row_start, key_span, 0)
        value_block = lax.dynamic_slice_in_dim(value_pad, row_start, key_span, 0)
        grad_block = lax.dynamic_slice_in_dim(grad_out, row_start, QBLOCK, 0)
        lse_block = lax.dynamic_slice_in_dim(log_sums, row_start, QBLOCK, 0)
        scores = band_scores(query_block, key_block, offset + row_start, seq_total)
        softmax_out = jnp.exp(scores - jnp.transpose(lse_block)[:, :, None])
        grad_probs = jnp.einsum(
            "qhd,khd->hqk", grad_block, value_block, preferred_element_type=jnp.float32
        )
        inner_sum = jnp.sum(softmax_out * grad_probs, -1, keepdims=True)
        grad_scores = (softmax_out * (grad_probs - inner_sum)).astype(jnp.bfloat16)
        query_grad = (
            jnp.einsum("hqk,khd->qhd", grad_scores, key_block, preferred_element_type=jnp.float32)
            * score_scale
        )
        key_part = (
            jnp.einsum("hqk,qhd->khd", grad_scores, query_block, preferred_element_type=jnp.float32)
            * score_scale
        )
        value_part = jnp.einsum(
            "hqk,qhd->khd",
            softmax_out.astype(jnp.bfloat16),
            grad_block,
            preferred_element_type=jnp.float32,
        )
        key_grads = lax.dynamic_update_slice_in_dim(
            key_grads,
            lax.dynamic_slice_in_dim(key_grads, row_start, key_span, 0) + key_part,
            row_start,
            0,
        )
        value_grads = lax.dynamic_update_slice_in_dim(
            value_grads,
            lax.dynamic_slice_in_dim(value_grads, row_start, key_span, 0) + value_part,
            row_start,
            0,
        )
        return ((key_grads, value_grads), query_grad)

    padded_zero = jnp.zeros(key_pad.shape, jnp.float32)
    carried, query_grads = lax.scan(
        one_block, (padded_zero, padded_zero), jnp.arange(row_count // QBLOCK, dtype=jnp.int32)
    )
    return (query_grads.reshape(queries.shape), carried[0], carried[1])


def shards(inputs, attn_gain, qkv_weight, proj_weight, mlp_gain, in_weight, out_weight, cotangent):
    gathered = (
        lax.all_gather(qkv_weight, "dp", axis=0, tiled=True),
        lax.all_gather(proj_weight, "dp", axis=0, tiled=True),
        lax.all_gather(in_weight, "dp", axis=0, tiled=True),
        lax.all_gather(out_weight, "dp", axis=0, tiled=True),
        lax.all_gather(attn_gain, "dp", axis=0, tiled=True),
        lax.all_gather(mlp_gain, "dp", axis=0, tiled=True),
    )
    qkv_full, proj_full, in_full, out_full, attn_full, mlp_full = gathered
    tokens = inputs.shape[0]
    seq_count = lax.axis_size("seq")
    seq_total = tokens * seq_count
    offset = lax.axis_index("seq") * tokens
    local_heads = HEADS // seq_count
    residual = inputs.astype(jnp.float32)
    normed_one, norm_one_back = jax.vjp(layer_norm, residual, attn_full.astype(jnp.float32))
    normed_low = normed_one.astype(jnp.bfloat16)
    projected = jnp.dot(normed_low, qkv_full, preferred_element_type=jnp.float32)
    positions = (offset + jnp.arange(tokens, dtype=jnp.int32)).astype(jnp.float32)
    cosine_table, sine_table = rotary_tables(positions, HEAD_DIM)

    def turn_pair(raw_pairs):
        return rotate(raw_pairs.reshape(tokens, 2 * HEADS, HEAD_DIM), cosine_table, sine_table)

    turned, turn_back = jax.vjp(turn_pair, projected[:, : 2 * D])
    query_low = turned[:, :HEADS].reshape(tokens, D).astype(jnp.bfloat16)
    key_low = turned[:, HEADS:].reshape(tokens, D).astype(jnp.bfloat16)
    value_low = projected[:, 2 * D :].astype(jnp.bfloat16)
    stacked = jnp.stack([query_low, key_low, value_low], 1)
    by_heads = lax.all_to_all(stacked, "seq", split_axis=2, concat_axis=0, tiled=True)
    head_queries = by_heads[:, 0].reshape(seq_total, local_heads, HEAD_DIM)
    keys_padded = jnp.pad(
        by_heads[:, 1].reshape(seq_total, local_heads, HEAD_DIM), ((WINDOW, WINDOW), (0, 0), (0, 0))
    )
    values_padded = jnp.pad(
        by_heads[:, 2].reshape(seq_total, local_heads, HEAD_DIM), ((WINDOW, WINDOW), (0, 0), (0, 0))
    )
    attended, log_sums = band_forward(head_queries, keys_padded, values_padded, 0, seq_total)
    attended_low = attended.astype(jnp.bfloat16).reshape(seq_total, D // seq_count)
    mixed_low = lax.all_to_all(attended_low, "seq", split_axis=0, concat_axis=1, tiled=True)
    attn_out = jnp.dot(mixed_low, proj_full, preferred_element_type=jnp.float32)
    hidden_state = residual + attn_out
    normed_two, norm_two_back = jax.vjp(layer_norm, hidden_state, mlp_full.astype(jnp.float32))
    normed_two_low = normed_two.astype(jnp.bfloat16)
    up_values = jnp.dot(normed_two_low, in_full, preferred_element_type=jnp.float32)
    gated, gated_back = jax.vjp(gated_gelu, up_values)
    gated_low = gated.astype(jnp.bfloat16)
    result = hidden_state + jnp.dot(gated_low, out_full, preferred_element_type=jnp.float32)
    output = result.astype(jnp.bfloat16)
    grad_result = cotangent.astype(jnp.float32)
    out_grad = jnp.einsum("tf,td->fd", gated_low, cotangent, preferred_element_type=jnp.float32)
    gated_grad = jnp.einsum("td,fd->tf", cotangent, out_full, preferred_element_type=jnp.float32)
    up_grad = gated_back(gated_grad)[0]
    up_low = up_grad.astype(jnp.bfloat16)
    in_grad = jnp.einsum("td,tf->df", normed_two_low, up_low, preferred_element_type=jnp.float32)
    normed_two_grad = jnp.einsum("tf,df->td", up_low, in_full, preferred_element_type=jnp.float32)
    hidden_part, mlp_gain_grad = norm_two_back(normed_two_grad)
    hidden_grad = grad_result + hidden_part
    attn_low = hidden_grad.astype(jnp.bfloat16)
    proj_grad = jnp.einsum("te,td->ed", mixed_low, attn_low, preferred_element_type=jnp.float32)
    mixed_grad = jnp.einsum(
        "td,ed->te", attn_low, proj_full, preferred_element_type=jnp.float32
    ).astype(jnp.bfloat16)
    grad_heads = lax.all_to_all(mixed_grad, "seq", split_axis=1, concat_axis=0, tiled=True)
    grad_heads = grad_heads.reshape(seq_total, local_heads, HEAD_DIM)
    query_grad, key_pad_grad, value_pad_grad = band_backward(
        head_queries, keys_padded, values_padded, grad_heads, log_sums, 0, seq_total
    )
    head_grads = jnp.stack(
        [
            query_grad.reshape(seq_total, D // seq_count),
            key_pad_grad[WINDOW : WINDOW + seq_total].reshape(seq_total, D // seq_count),
            value_pad_grad[WINDOW : WINDOW + seq_total].reshape(seq_total, D // seq_count),
        ],
        1,
    ).astype(jnp.bfloat16)
    token_grads = lax.all_to_all(head_grads, "seq", split_axis=0, concat_axis=2, tiled=True)
    rotated_grad = jnp.concatenate(
        [
            token_grads[:, 0].reshape(tokens, HEADS, HEAD_DIM),
            token_grads[:, 1].reshape(tokens, HEADS, HEAD_DIM),
        ],
        1,
    ).astype(jnp.float32)
    raw_grad = turn_back(rotated_grad)[0]
    proj_in_grad = jnp.concatenate([raw_grad, token_grads[:, 2].astype(jnp.float32)], 1).astype(
        jnp.bfloat16
    )
    qkv_grad = jnp.einsum("td,tf->df", normed_low, proj_in_grad, preferred_element_type=jnp.float32)
    normed_grad = jnp.einsum(
        "tf,df->td", proj_in_grad, qkv_full, preferred_element_type=jnp.float32
    )
    input_part, attn_gain_grad = norm_one_back(normed_grad)
    input_grad = (hidden_grad + input_part).astype(jnp.bfloat16)
    shares = (
        lax.psum_scatter(qkv_grad, "dp", scatter_dimension=0, tiled=True),
        lax.psum_scatter(proj_grad, "dp", scatter_dimension=0, tiled=True),
        lax.psum_scatter(in_grad, "dp", scatter_dimension=0, tiled=True),
        lax.psum_scatter(out_grad, "dp", scatter_dimension=0, tiled=True),
        lax.psum_scatter(attn_gain_grad, "dp", scatter_dimension=0, tiled=True),
        lax.psum_scatter(mlp_gain_grad, "dp", scatter_dimension=0, tiled=True),
    )
    totals = (
        lax.psum(shares[0].astype(jnp.bfloat16), "seq").astype(jnp.float32),
        lax.psum(shares[1].astype(jnp.bfloat16), "seq").astype(jnp.float32),
        lax.psum(shares[2].astype(jnp.bfloat16), "seq").astype(jnp.float32),
        lax.psum(shares[3].astype(jnp.bfloat16), "seq").astype(jnp.float32),
        lax.psum(shares[4].astype(jnp.bfloat16), "seq").astype(jnp.float32),
        lax.psum(shares[5].astype(jnp.bfloat16), "seq").astype(jnp.float32),
    )
    return (output, input_grad, totals[4], totals[0], totals[1], totals[5], totals[2], totals[3])


def solution(mesh):
    in_specs = (
        P(("dp", "seq"), None),
        P("dp"),
        P("dp", None),
        P("dp", None),
        P("dp"),
        P("dp", None),
        P("dp", None),
        P(("dp", "seq"), None),
    )
    out_specs = (
        P(("dp", "seq"), None),
        P(("dp", "seq"), None),
        P("dp"),
        P("dp", None),
        P("dp", None),
        P("dp"),
        P("dp", None),
        P("dp", None),
    )
    return jax.shard_map(shards, mesh=mesh, in_specs=in_specs, out_specs=out_specs, check_vma=False)
```

profile of v0, /device:TPU:0, one launch (start us, length us, event | category | flops | bytes accessed | tf_op | source)
XLA Modules:
  0.0 997.3 jit_solution(2272519886768296588)
XLA Ops:
  11.6 15.3 %all-reduce.11 = (bf16[768]{0:T(1024)(128)(2,1)S(1)}, bf16[768]{0:T(1024)(128)(2,1)S(1)}) all-reduce(bf16[768]{0:T(1024)(128)(2,1)S(1)} %dynamic-update-slice, bf16[768]{0:T(1024)(128)(2,1)S(1)} %dynamic-update-slice.1), channel_id=1, replica_groups=mesh['dp'=8,'seq'=4] {'dp'}, use_global_device_ids=true, to_apply=%add.6 | all-reduce | flops 1536 | bytes 6144
  29.0 17.7 %all-gather.5.cloned.1.call-done = bf16[768,2304]{1,0:T(8,128)(2,1)} async-done(((bf16[96,2304]{1,0:T(8,128)(2,1)}), bf16[768,2304]{1,0:T(8,128)(2,1)}) %all-gather.5.cloned.1.call-update) | async-done | bytes 3538960 | tf_op jit(solution)/shard_map/all_gather | solution.py:138
  46.7 6.2 fusion.81
  52.9 3.6 slice.69
  56.7 6.6 copy.55
  63.2 3.7 slice_negate_fusion.1
  77.0 3.8 pad_maximum_fusion
  80.8 11.1 %copy.58 = bf16[1024,3,768]{0,1,2:T(4,128)(2,1)} copy(bf16[1024,3,768]{2,0,1:T(8,128)(2,1)} %pad_maximum_fusion) | data formatting | bytes 9437184 | tf_op jit(solution)/shard_map/stack | solution.py:165
  91.9 5.2 all-to-all-start
  98.6 137.3 %all-to-all-done = bf16[1024,3,768]{0,1,2:T(4,128)(2,1)} async-done(((bf16[1024,3,768]{0,1,2:T(4,128)(2,1)}), bf16[1024,3,768]{0,1,2:T(4,128)(2,1)}, u32[]{:S(2)}, u32[]{:S(2)}) %all-to-all-start) | async-done | bytes 4718624 | tf_op jit(solution)/shard_map/all_to_all | solution.py:166
  236.0 4.7 copy.59
  246.6 67.9 %while.30 = (s32[]{:T(128)}, bf16[8,512,3,64]{1,3,2,0:T(8,128)(2,1)}, f32[8,512,3]{1,2,0:T(4,128)}, s32[8]{0:T(128)S(1)}, bf16[4224,3,64]{0,2,1:T(8,128)(2,1)}, ...) while((s32[]{:T(128)}, ...), condition=%wide.region_5.6_spmd, body=%wide.region_2.5_spmd.sunk | while | flops 265094656 | bytes 14252788 | solution.py:77
  251.9 3.1 fusion.143
  260.4 3.1 fusion.143
  268.9 3.1 fusion.143
  277.3 3.1 fusion.143
  285.8 3.1 fusion.143
  294.3 3.1 fusion.143
  302.8 3.1 fusion.143
  311.3 3.1 fusion.143
  314.4 3.4 copy.61
  317.8 3.7 convert_element_type.147
  324.6 4.4 all-to-all-start.1
  332.6 33.3 %all-to-all-done.1 = bf16[4,1024,192]{1,2,0:T(8,128)(2,1)} async-done(((bf16[4,1024,192]{1,2,0:T(8,128)(2,1)}), bf16[4,1024,192]{1,2,0:T(8,128)(2,1)}, u32[]{:S(2)}, u32[]{:S(2)}) %all-to-all-start.1) | async-done | bytes 1572896 | tf_op jit(solution)/shard_map/all_to_all | solution.py:176
  365.9 3.3 fusion.97
  371.3 10.7 %fusion.89 = f32[1024,2304]{1,0:T(8,128)} fusion(bf16[768,2304]{1,0:T(8,128)(2,1)} %all-gather.9.cloned.1.call-done, f32[1024,768]{0,1:T(8,128)} %copy-done.6, f32[768]{0:T(1024)S(1)} %convert_element_type.148, f32[1024]{0:T(1024)S(1)} %fusion.84, f32[1024]{0:T(1024)S(1)} %broadcast_multiply_fusion), kind=kOutput, calls=%fused_computation.152 | convolution fusion | flops 3627024384 | bytes 16133120 | tf_op jit(solution)/shard_map/dot_general | solution.py:181
  382.0 14.9 %fusion.76 = (f32[1024,1152]{1,0:T(8,128)}, f32[1024,1152]{1,0:T(8,128)S(1)}, f32[1024,1152]{1,0:T(8,128)S(1)}) fusion(f32[1024,2304]{1,0:T(8,128)} %fusion.89, bf16[1024,768]{1,0:T(8,128)(2,1)S(1)} %copy-done.15, bf16[1152,768]{1,0:T(8,128)(2,1)} %all-gather.11.cloned.1.call-done), kind=kOutput, calls=%fused_computation.125 | convolution fusion | flops 1888616448 | bytes 22216704 | tf_op jit(solution)/shard_map/td,fd->tf/dot_general | solution.py:188
  396.9 3.5 multiply_add_fusion
  400.4 9.0 multiply_reduce_fusion.1
  413.0 4.3 fusion.98
  417.4 5.6 fusion.99
  424.5 3.9 convolution_convert_fusion
  428.4 3.6 all-to-all-start.2
  432.0 11.4 %fusion.77 = f32[768,2304]{1,0:T(8,128)} fusion(f32[1024,1152]{1,0:T(8,128)} %copy-done.9, f32[1024,1152]{1,0:T(8,128)} %get-tuple-element.312, f32[1024,768]{0,1:T(8,128)} %copy-done.6, f32[768]{0:T(1024)S(1)} %convert_element_type.148, f32[1024]{0:T(1024)S(1)} %fusion.84, f32[1024]{0:T(1024)S(1)} %broadcast_multiply_fusion), kind=kOutput, calls=%fused_computation.126 | convolution fusion | flops 3631742976 | bytes 19672064 | tf_op jit(solution)/shard_map/td,tf->df/dot_general | solution.py:191
  443.5 24.9 %all-to-all-done.2 = bf16[1024,4,192]{0,2,1:T(8,128)(2,1)S(1)} async-done(((bf16[1024,4,192]{0,2,1:T(8,128)(2,1)}), bf16[1024,4,192]{0,2,1:T(8,128)(2,1)S(1)}, u32[]{:S(2)}, u32[]{:S(2)}) %all-to-all-start.2) | async-done | bytes 1572896 | tf_op jit(solution)/shard_map/all_to_all | solution.py:200
  479.1 134.9 %while.31 = (s32[]{:T(128)}, f32[4224,3,64]{0,2,1:T(8,128)}, f32[4224,3,64]{0,2,1:T(8,128)}, bf16[8,512,3,64]{1,3,2,0:T(8,128)(2,1)}, s32[8]{0:T(128)S(1)}, /*in...) while((s32[]{:T(128)}, f32[4224,3,64]{0,2,1:T(8,128)}, ...), condition=%wide.region_12.13_spmd, body=%wide.region_10.12_spmd.sunk | while | flops 640099840 | bytes 49803588 | solution.py:130
  480.4 3.5 fusion.152
  485.2 4.0 multiply_reduce_fusion.5
  497.2 3.5 fusion.152
  502.0 4.0 multiply_reduce_fusion.5
  514.0 3.5 fusion.152
  518.7 4.2 multiply_reduce_fusion.5
  531.0 3.5 fusion.152
  535.8 4.1 multiply_reduce_fusion.5
  548.3 3.5 fusion.152
  553.0 4.0 multiply_reduce_fusion.5
  565.1 3.5 fusion.152
  569.8 4.0 multiply_reduce_fusion.5
  581.8 3.5 fusion.152
  586.6 4.0 multiply_reduce_fusion.5
  598.6 3.5 fusion.152
  603.3 4.0 multiply_reduce_fusion.5
  624.4 12.8 %copy.67 = bf16[4096,3,192]{2,1,0:T(4,128)(2,1)} copy(bf16[4096,3,192]{0,2,1:T(8,128)(2,1)} %pad_maximum_fusion.1) | data formatting | bytes 9437184 | tf_op jit(solution)/shard_map/stack | solution.py:205
  637.2 190.6 %all_to_all.68 = bf16[4096,3,192]{2,1,0:T(4,128)(2,1)} all-to-all(bf16[4096,3,192]{2,1,0:T(4,128)(2,1)} %copy.67), channel_id=1, replica_groups=mesh['dp'=8,'seq'=4] {'seq'}, dimensions={0} | all-to-all | bytes 9437184 | tf_op jit(solution)/shard_map/all_to_all | solution.py:213
  827.8 12.8 %copy.69 = bf16[1024,3,4,192]{0,3,2,1:T(8,128)(2,1)} copy(bf16[1024,3,4,192]{3,1,0,2:T(4,128)(2,1)} %bitcast.117) | data formatting | bytes 9437184 | tf_op jit(solution)/shard_map/all_to_all | solution.py:213
  848.8 7.7 fusion.72
  857.2 6.7 add_convert_fusion.2
  870.4 8.6 fusion.71
  881.4 38.9 %reduce-scatter.5.cloned.1.call-done = f32[96,2304]{1,0:T(8,128)} async-done(((f32[768,2304]{1,0:T(8,128)}), f32[96,2304]{1,0:T(8,128)}) %reduce-scatter.5.cloned.1.call-update) | async-done | bytes 884752 | tf_op jit(solution)/shard_map/reduce_scatter | solution.py:232
  922.3 3.3 fusion.69
  925.6 13.4 %all-reduce.10 = (bf16[768]{0:T(1024)(128)(2,1)S(1)}, bf16[768]{0:T(1024)(128)(2,1)S(1)}) all-reduce(f32[768]{0:T(1024)S(1)} %get-tuple-element.264, f32[768]{0:T(1024)S(1)} %get-tuple-element.262), channel_id=2, replica_groups=mesh['dp'=8,'seq'=4] {'dp'}, use_global_device_ids=true, to_apply=%region_16.17.clone | all-reduce | flops 1536 | bytes 9216
  939.1 12.3 %all-reduce.12 = (bf16[96]{0:T(256)(128)(2,1)S(1)}, bf16[96]{0:T(256)(128)(2,1)S(1)}) all-reduce(bf16[96]{0:T(256)(128)(2,1)S(1)} %dynamic-slice.9, bf16[96]{0:T(256)(128)(2,1)S(1)} %dynamic-slice.8), channel_id=1, replica_groups=mesh['dp'=8,'seq'=4] {'seq'}, use_global_device_ids=true, to_apply=%region_17.18 | all-reduce | flops 192 | bytes 768 | tf_op jit(solution)/shard_map/psum | solution.py:244
  952.4 5.5 add_convert_fusion.1
  960.5 23.2 %all-reduce.16.cloned.1.call-done = (bf16[96,2304]{1,0:T(8,128)(2,1)}, bf16[96,768]{1,0:T(8,128)(2,1)}, bf16[96,2304]{1,0:T(8,128)(2,1)}, bf16[144,768]{1,0:T(8,128)(2,1)}) async-done(((bf16[96,2304]{1,0:T(8,128)(2,1)}, bf16[96,768]{1,0:T(8,128)(2,1)}, bf16[96,2304]{1,0:T(8,128)(2,1)}, bf16[144,768]{1,0:T(8,128)(2,1)}), (bf16[96,2304]{1,0:T(8,128)(2,1)}, bf16[96,768]{1,0:T(8,128)(2,1)}, ...) | async-done | bytes 1253392 | tf_op jit(solution)/shard_map/psum | solution.py:240
  (315 shorter events, 193.9 us)
Async XLA Ops:
  7.2 2.5 copy-start.27
  7.2 3.9 copy-start.28
  7.2 4.1 copy-start.29
  7.2 39.5 %all-gather.5.cloned.1.call-start = ((), (), s32[]{:S(2)}) async-start(), calls=%async_computation.8 | async-start | bytes 3981312 | tf_op jit(solution)/shard_map/all_gather | solution.py:138
  9.7 356.2 %copy-start.1 = (bf16[1024,768]{0,1:T(8,128)(2,1)}, bf16[1024,768]{0,1:T(8,128)(2,1)S(1)}, u32[]{:S(2)}) copy-start(bf16[1024,768]{0,1:T(8,128)(2,1)S(1)} %copy.54) | copy-start | bytes 4718596
  26.9 26.0 %copy-start.21 = (f32[768]{0:T(1024)}, f32[768]{0:T(1024)S(1)}, u32[]{:S(2)}) copy-start(f32[768]{0:T(1024)S(1)} %convert_element_type.141) | copy-start | bytes 9220
  28.2 38.7 %copy-start.11 = (f32[1024,64]{0,1:T(8,128)}, f32[1024,64]{0,1:T(8,128)S(1)}, u32[]{:S(2)}) copy-start(f32[1024,64]{0,1:T(8,128)S(1)} %get-tuple-element.346) | copy-start | bytes 786436
  28.5 24.4 %copy-start.19 = (f32[1024]{0:T(1024)}, f32[1024]{0:T(1024)S(1)}, u32[]{:S(2)}) copy-start(f32[1024]{0:T(1024)S(1)} %broadcast_multiply_fusion.1) | copy-start | bytes 12292
  29.0 23.9 %copy-start.25 = (f32[1024]{0:T(1024)}, f32[1024]{0:T(1024)S(1)}, u32[]{:S(2)}) copy-start(f32[1024]{0:T(1024)S(1)} %fusion.70) | copy-start | bytes 12292
  29.0 23.9 %copy-start.23 = (f32[1024]{0:T(1024)}, f32[1024]{0:T(1024)S(1)}, u32[]{:S(2)}) copy-start(f32[1024]{0:T(1024)S(1)} %fusion.83) | copy-start | bytes 12292
  63.2 4.0 slice-start
  63.2 4.7 slice-start.1
  63.2 4.7 copy-start.13
  91.9 144.1 %all-to-all-start = ((bf16[1024,3,768]{0,1,2:T(4,128)(2,1)}), bf16[1024,3,768]{0,1,2:T(4,128)(2,1)}, u32[]{:S(2)}, u32[]{:S(2)}) async-start(bf16[1024,3,768]{0,1,2:T(4,128)(2,1)} %copy.58), calls=%async_computation | async-start | bytes 12582912 | tf_op jit(solution)/shard_map/all_to_all | solution.py:166
  97.1 235.5 %all-gather.7.cloned.1.call-start = ((), (), s32[]{:S(2)}) async-start(), calls=%async_computation.9 | async-start | bytes 1327104 | tf_op jit(solution)/shard_map/all_gather | solution.py:139
  97.9 273.4 %all-gather.9.cloned.1.call-start = ((), (), s32[]{:S(2)}) async-start(), calls=%async_computation.10 | async-start | bytes 3981312 | tf_op jit(solution)/shard_map/all_gather | solution.py:140
  324.6 41.3 %all-to-all-start.1 = ((bf16[4,1024,192]{1,2,0:T(8,128)(2,1)}), bf16[4,1024,192]{1,2,0:T(8,128)(2,1)}, u32[]{:S(2)}, u32[]{:S(2)}) async-start(bf16[4,1024,192]{1,2,0:T(8,128)(2,1)} %copy.62), calls=%async_computation.1 | async-start | bytes 3145728 | tf_op jit(solution)/shard_map/all_to_all | solution.py:176
  329.0 53.1 %all-gather.11.cloned.1.call-start = ((), (), s32[]{:S(2)}) async-start(), calls=%async_computation.11 | async-start | bytes 1990656 | tf_op jit(solution)/shard_map/all_gather | solution.py:141
  329.5 537.4 %reduce-scatter.7.cloned.1.call-start = ((), (), s32[]{:S(2)}) async-start(), calls=%async_computation.13 | async-start | bytes 2654208 | tf_op jit(solution)/shard_map/reduce_scatter | solution.py:233
  369.1 1.7 copy-start.6
  371.3 10.8 %copy-start.15 = (bf16[1024,768]{1,0:T(8,128)(2,1)S(1)}, bf16[1024,768]{1,0:T(8,128)(2,1)}, u32[]{:S(2)}) copy-start(bf16[1024,768]{1,0:T(8,128)(2,1)} %param.19) | copy-start | bytes 4718596
  382.0 14.9 %copy-start.8 = (f32[1024,2304]{1,0:T(8,128)S(1)}, f32[1024,2304]{1,0:T(8,128)}, u32[]{:S(2)}) copy-start(f32[1024,2304]{1,0:T(8,128)} %fusion.89) | copy-start | bytes 28311556
  396.9 3.5 copy-start.7
  400.4 9.0 copy-start.9
  409.4 1.4 copy-start.4
  410.2 1.6 copy-start.3
  411.9 1.1 copy-start.16
  417.3 451.3 %reduce-scatter.11.cloned.1.call-start = ((), (), s32[]{:S(2)}) async-start(), calls=%async_computation.15 | async-start | bytes 3981312 | tf_op jit(solution)/shard_map/reduce_scatter | solution.py:235
  423.0 1.5 copy-start.17
  428.4 40.0 %all-to-all-start.2 = ((bf16[1024,4,192]{0,2,1:T(8,128)(2,1)}), bf16[1024,4,192]{0,2,1:T(8,128)(2,1)S(1)}, u32[]{:S(2)}, u32[]{:S(2)}) async-start(bf16[1024,4,192]{0,2,1:T(8,128)(2,1)} %bitcast.135), calls=%async_computation.2 | async-start | bytes 3145728 | tf_op jit(solution)/shard_map/all_to_all | solution.py:200
  431.9 447.2 %reduce-scatter.9.cloned.1.call-start = ((), (), s32[]{:S(2)}) async-start(), calls=%async_computation.14 | async-start | bytes 7962624 | tf_op jit(solution)/shard_map/reduce_scatter | solution.py:234
  443.4 476.9 %reduce-scatter.5.cloned.1.call-start = ((), (), s32[]{:S(2)}) async-start(), calls=%async_computation.12 | async-start | bytes 7962624 | tf_op jit(solution)/shard_map/reduce_scatter | solution.py:232
  485.2 4.0 copy-start
  502.0 4.0 copy-start
  518.7 4.2 copy-start
  535.8 4.5 copy-start
  553.0 4.0 copy-start
  569.8 4.0 copy-start
  586.6 4.0 copy-start
  603.3 4.0 copy-start
  840.6 2.9 copy-start.14
  844.4 1.3 copy-start.12
  845.7 3.2 copy-start.2
  845.7 3.2 copy-start.20
  845.7 3.1 copy-start.22
  845.7 3.1 copy-start.24
  847.1 1.7 copy-start.10
  856.5 127.2 %all-reduce.16.cloned.1.call-start = ((), (), s32[]{:S(2)}) async-start(), calls=%async_computation.16 | async-start | bytes 2506752 | tf_op jit(solution)/shard_map/psum | solution.py:240
  870.4 8.6 copy-start.26
  922.3 30.1 %copy-start.5 = (bf16[1024,768]{0,1:T(8,128)(2,1)S(1)}, bf16[1024,768]{0,1:T(8,128)(2,1)}, u32[]{:S(2)}) copy-start(bf16[1024,768]{0,1:T(8,128)(2,1)} %copy.64) | copy-start | bytes 4718596
  983.8 5.7 copy-start.18
Sparse Core Ops, SparseCore 0:
  9.9 36.7 all-gather.4
  99.8 24.4 all-gather.6
  126.3 33.9 all-gather.8
  331.4 26.9 all-gather.10
  417.5 40.6 reduce-scatter.6
  461.8 48.0 reduce-scatter.10
  513.9 65.5 reduce-scatter.8
  856.7 63.5 reduce-scatter.4
  923.7 59.9 all-reduce.15
where the time goes:
time: 1010 us; the launch traced here: 997 us
  waiting for transfers between devices  278 us (28%)
  matrix products  244 us (24%)
  blocking collectives  232 us (23%)
  local copies, waits for them, and re-layouts  131 us (13%)
  other arithmetic  72 us (7%)
  between operations  16.2 us (2%)
  starting transfers between devices  14.1 us (1%)
  loops' own time  10.6 us (1%)
    all_to_all x1, blocking collectives, shards(): lax.all_to_all(head_grads, 'seq', split_axis=0, concat_axis=2, tiled=True)  191 us
    all_to_all x1, waiting for transfers between devices, shards(): lax.all_to_all(stacked, 'seq', split_axis=2, concat_axis=0, tiled=True)  137 us
    dot_general x16, matrix products, band_scores(): jnp.einsum('qhd,khd->hqk', query_block, key_block, preferred_element_type...  48.2 us
    reduce_scatter x1, waiting for transfers between devices, shards(): lax.psum_scatter(qkv_grad, 'dp', scatter_dimension=0, tiled=True)  38.9 us
    all_to_all x1, waiting for transfers between devices, shards(): lax.all_to_all(attended_low, 'seq', split_axis=0, concat_axis=1, tiled=True)  33.3 us
    unnamed x2, blocking collectives  28.7 us
    dot_general x8, matrix products, one_block(): jnp.einsum('qhd,khd->hqk', grad_block, value_block, preferred_element_typ...  28.3 us
    dot_general x8, matrix products, one_block(): jnp.einsum('hqk,khd->qhd', softmax_low, value_block, preferred_element_ty...  25.1 us
  transfers between devices with their start and end apart: 12, of which 6 were waited for; matrix products, arithmetic and copies ran while one was open for 35% of the time, Pallas kernels for 0%

commit v1 on v0

--- a/solution.py
+++ b/solution.py
@@ -12,6 +12,28 @@
 epsilon = 1e-05
 theta_base = 10000.0
 masked_score = -1e30
+
+
+def split_up(x, dim, size):
+    before, after = (x.shape[:dim], x.shape[dim + 1 :])
+    return jnp.moveaxis(x.reshape(*before, size, -1, *after), dim, 0)
+
+
+def joined_along(blocks, dim):
+    blocks = jnp.moveaxis(blocks, 0, dim)
+    lengths = blocks.shape
+    return blocks.reshape(*lengths[:dim], lengths[dim] * lengths[dim + 1], *lengths[dim + 2 :])
+
+
+def rotated_exchange(x, axis, split_dim, concat_dim):
+    peers, place = (lax.axis_size(axis), lax.axis_index(axis))
+    blocks = split_up(x, split_dim, peers)
+    done = [blocks[place]]
+    for step in range(1, peers):
+        sent = blocks[(place + step) % peers]
+        done.append(lax.ppermute(sent, axis, [(i, (i + step) % peers) for i in range(peers)]))
+    blocks = jnp.stack(done)[(place - jnp.arange(peers)) % peers]
+    return joined_along(blocks, concat_dim)
 
 
 def layer_norm(features, gain_vector):
@@ -210,7 +232,7 @@
         ],
         1,
     ).astype(jnp.bfloat16)
-    token_grads = lax.all_to_all(head_grads, "seq", split_axis=0, concat_axis=2, tiled=True)
+    token_grads = rotated_exchange(head_grads, "seq", 0, 2)
     rotated_grad = jnp.concatenate(
         [
             token_grads[:, 0].reshape(tokens, HEADS, HEAD_DIM),

time: 1010 us -> 913 us (0.904)
  blocking collectives: 232 us -> 41 us
  waiting for transfers between devices: 278 us -> 378 us
    all_to_all x1 -> x0, blocking collectives: 191 us -> none  [shards(): lax.all_to_all(head_grads, 'seq', split_axis=0, concat_axis=2, tiled=True)]
    ppermute x0 -> x3, waiting for transfers between devices: none -> 75.8 us  [rotated_exchange(): lax.ppermute(sent, axis, [(i, (i + step) % peers) for i in range(peers)])]
    reduce_scatter x1, waiting for transfers between devices: 38.9 us -> 63.2 us  [shards(): lax.psum_scatter(qkv_grad, 'dp', scatter_dimension=0, tiled=True)]
    all_to_all x1 -> x0, local copies, waits for them, and re-layouts: 12.8 us -> none  [shards(): lax.all_to_all(head_grads, 'seq', split_axis=0, concat_axis=2, tiled=True)]
    unnamed x73 -> x77, local copies, waits for them, and re-layouts: 19.4 us -> 21.1 us
  transfers between devices with their start and end apart: 12 -> 15, of which waited for: 6 -> 8; matrix products, arithmetic and copies ran while one was open for 35% -> 38% of each run, Pallas kernels for 0% -> 0%
where the time goes in v1:
time: 913 us; the launch traced here: 901 us
  waiting for transfers between devices  378 us (41%)
  matrix products  244 us (27%)
  local copies, waits for them, and re-layouts  123 us (13%)
  other arithmetic  71.3 us (8%)
  blocking collectives  41 us (4%)
  starting transfers between devices  18.1 us (2%)
  between operations  16 us (2%)
  loops' own time  9.83 us (1%)
    all_to_all x1, waiting for transfers between devices, shards(): lax.all_to_all(stacked, 'seq', split_axis=2, concat_axis=0, tiled=True)  137 us
    ppermute x3, waiting for transfers between devices, rotated_exchange(): lax.ppermute(sent, axis, [(i, (i + step) % peers) for i in range(peers)])  75.8 us
    reduce_scatter x1, waiting for transfers between devices, shards(): lax.psum_scatter(qkv_grad, 'dp', scatter_dimension=0, tiled=True)  63.2 us
    dot_general x16, matrix products, band_scores(): jnp.einsum('qhd,khd->hqk', query_block, key_block, preferred_element_type...  48.5 us
    all_to_all x1, waiting for transfers between devices, shards(): lax.all_to_all(attended_low, 'seq', split_axis=0, concat_axis=1, tiled=True)  33.5 us
    dot_general x8, matrix products, one_block(): jnp.einsum('qhd,khd->hqk', grad_block, value_block, preferred_element_typ...  28.8 us
    unnamed x2, blocking collectives  28.7 us
    dot_general x8, matrix products, one_block(): jnp.einsum('hqk,khd->qhd', softmax_low, value_block, preferred_element_ty...  25.1 us
  transfers between devices with their start and end apart: 15, of which 8 were waited for; matrix products, arithmetic and copies ran while one was open for 38% of the time, Pallas kernels for 0%

profile of v1, /device:TPU:0, one launch (start us, length us, event | category | flops | bytes accessed | tf_op | source)
XLA Modules:
  0.0 901.4 jit_solution(8948427698868536293)
XLA Ops:
  11.6 15.3 %all-reduce.11 = (bf16[768]{0:T(1024)(128)(2,1)S(1)}, bf16[768]{0:T(1024)(128)(2,1)S(1)}) all-reduce(bf16[768]{0:T(1024)(128)(2,1)S(1)} %dynamic-update-slice, bf16[768]{0:T(1024)(128)(2,1)S(1)} %dynamic-update-slice.1), channel_id=1, replica_groups=mesh['dp'=8,'seq'=4] {'dp'}, use_global_device_ids=true, to_apply=%add.6 | all-reduce | flops 1536 | bytes 6144
  29.0 17.7 %all-gather.5.cloned.1.call-done = bf16[768,2304]{1,0:T(8,128)(2,1)} async-done(((bf16[96,2304]{1,0:T(8,128)(2,1)}), bf16[768,2304]{1,0:T(8,128)(2,1)}) %all-gather.5.cloned.1.call-update) | async-done | bytes 3538960 | tf_op jit(solution)/shard_map/all_gather | solution.py:160
  46.7 6.2 fusion.81
  52.9 3.7 slice.71
  56.7 6.6 copy.57
  63.3 3.7 slice_negate_fusion.1
  77.0 3.8 pad_maximum_fusion
  80.8 11.1 %copy.60 = bf16[1024,3,768]{0,1,2:T(4,128)(2,1)} copy(bf16[1024,3,768]{2,0,1:T(8,128)(2,1)} %pad_maximum_fusion) | data formatting | bytes 9437184 | tf_op jit(solution)/shard_map/stack | solution.py:187
  91.8 5.3 all-to-all-start
  98.7 137.3 %all-to-all-done = bf16[1024,3,768]{0,1,2:T(4,128)(2,1)} async-done(((bf16[1024,3,768]{0,1,2:T(4,128)(2,1)}), bf16[1024,3,768]{0,1,2:T(4,128)(2,1)}, u32[]{:S(2)}, u32[]{:S(2)}) %all-to-all-start) | async-done | bytes 4718624 | tf_op jit(solution)/shard_map/all_to_all | solution.py:188
  236.0 4.7 copy.61
  246.6 68.3 %while.30 = (s32[]{:T(128)}, bf16[8,512,3,64]{1,3,2,0:T(8,128)(2,1)}, f32[8,512,3]{1,2,0:T(4,128)}, s32[8]{0:T(128)S(1)}, bf16[4224,3,64]{0,2,1:T(8,128)(2,1)}, ...) while((s32[]{:T(128)}, ...), condition=%wide.region_5.6_spmd, body=%wide.region_2.5_spmd.sunk | while | flops 265094656 | bytes 14252788 | solution.py:99
  260.6 3.1 fusion.145
  269.1 3.1 fusion.145
  294.7 3.1 fusion.145
  303.3 3.1 fusion.145
  315.0 3.4 copy.63
  318.4 3.7 convert_element_type.148
  325.1 4.3 all-to-all-start.1
  332.9 33.5 %all-to-all-done.1 = bf16[4,1024,192]{1,2,0:T(8,128)(2,1)} async-done(((bf16[4,1024,192]{1,2,0:T(8,128)(2,1)}), bf16[4,1024,192]{1,2,0:T(8,128)(2,1)}, u32[]{:S(2)}, u32[]{:S(2)}) %all-to-all-start.1) | async-done | bytes 1572896 | tf_op jit(solution)/shard_map/all_to_all | solution.py:198
  366.4 3.3 fusion.99
  371.8 10.7 %fusion.91 = f32[1024,2304]{1,0:T(8,128)} fusion(bf16[768,2304]{1,0:T(8,128)(2,1)} %all-gather.9.cloned.1.call-done, f32[1024,768]{0,1:T(8,128)} %copy-done.6, f32[768]{0:T(1024)S(1)} %convert_element_type.149, f32[1024]{0:T(1024)S(1)} %fusion.84, f32[1024]{0:T(1024)S(1)} %broadcast_multiply_fusion), kind=kOutput, calls=%fused_computation.167 | convolution fusion | flops 3627024384 | bytes 16133120 | tf_op jit(solution)/shard_map/dot_general | solution.py:203
  382.5 14.9 %fusion.76 = (f32[1024,1152]{1,0:T(8,128)}, f32[1024,1152]{1,0:T(8,128)S(1)}, f32[1024,1152]{1,0:T(8,128)S(1)}) fusion(f32[1024,2304]{1,0:T(8,128)} %fusion.91, bf16[1024,768]{1,0:T(8,128)(2,1)S(1)} %copy-done.16, bf16[1152,768]{1,0:T(8,128)(2,1)} %all-gather.11.cloned.1.call-done), kind=kOutput, calls=%fused_computation.129 | convolution fusion | flops 1888616448 | bytes 22216704 | tf_op jit(solution)/shard_map/td,fd->tf/dot_general | solution.py:210
  397.4 3.6 multiply_add_fusion
  401.0 9.0 multiply_reduce_fusion.1
  413.6 4.2 fusion.100
  417.9 5.5 fusion.101
  424.9 3.9 convolution_convert_fusion
  428.8 3.6 all-to-all-start.2
  432.5 11.5 %fusion.77 = f32[768,2304]{1,0:T(8,128)} fusion(f32[1024,1152]{1,0:T(8,128)} %copy-done.10, f32[1024,1152]{1,0:T(8,128)} %get-tuple-element.312, f32[1024,768]{0,1:T(8,128)} %copy-done.6, f32[768]{0:T(1024)S(1)} %convert_element_type.149, f32[1024]{0:T(1024)S(1)} %fusion.84, f32[1024]{0:T(1024)S(1)} %broadcast_multiply_fusion), kind=kOutput, calls=%fused_computation.133 | convolution fusion | flops 3631742976 | bytes 19672064 | tf_op jit(solution)/shard_map/td,tf->df/dot_general | solution.py:213
  444.0 24.7 %all-to-all-done.2 = bf16[1024,4,192]{0,2,1:T(8,128)(2,1)S(1)} async-done(((bf16[1024,4,192]{0,2,1:T(8,128)(2,1)}), bf16[1024,4,192]{0,2,1:T(8,128)(2,1)S(1)}, u32[]{:S(2)}, u32[]{:S(2)}) %all-to-all-start.2) | async-done | bytes 1572896 | tf_op jit(solution)/shard_map/all_to_all | solution.py:222
  471.1 3.3 reshape.371
  479.5 134.3 %while.31 = (s32[]{:T(128)}, f32[4224,3,64]{0,2,1:T(8,128)}, f32[4224,3,64]{0,2,1:T(8,128)}, bf16[8,512,3,64]{1,3,2,0:T(8,128)(2,1)}, s32[8]{0:T(128)S(1)}, /*in...) while((s32[]{:T(128)}, f32[4224,3,64]{0,2,1:T(8,128)}, ...), condition=%wide.region_12.13_spmd, body=%wide.region_10.12_spmd.sunk | while | flops 640099840 | bytes 49803588 | solution.py:152
  480.7 3.6 fusion.154
  485.5 4.0 multiply_reduce_fusion.5
  497.3 3.6 fusion.154
  502.2 4.1 multiply_reduce_fusion.5
  514.0 3.6 fusion.154
  518.9 4.6 multiply_reduce_fusion.5
  531.4 3.6 fusion.154
  536.3 4.1 multiply_reduce_fusion.5
  548.4 3.6 fusion.154
  553.2 4.0 multiply_reduce_fusion.5
  565.1 3.6 fusion.154
  569.9 4.0 multiply_reduce_fusion.5
  581.7 3.6 fusion.154
  586.6 4.0 multiply_reduce_fusion.5
  598.4 3.6 fusion.154
  603.2 4.0 multiply_reduce_fusion.5
  617.2 3.6 slice.111
  623.6 3.6 slice.110
  627.2 3.9 stack.33
  637.4 26.9 %collective-permute-done = bf16[1024,3,192]{0,2,1:T(8,128)(2,1)S(1)} collective-permute-done((bf16[1024,3,192]{0,2,1:T(8,128)(2,1)S(1)}, bf16[1024,3,192]{0,2,1:T(8,128)(2,1)S(1)}, u32[]{:S(2)}, u32[]{:S(2)}) %collective-permute-start) | collective-permute-done | bytes 1179680 | tf_op jit(solution)/shard_map/ppermute | solution.py:34
  664.3 48.8 %collective-permute-done.1 = bf16[1024,3,192]{0,2,1:T(8,128)(2,1)S(1)} collective-permute-done((bf16[1024,3,192]{0,2,1:T(8,128)(2,1)S(1)}, bf16[1024,3,192]{0,2,1:T(8,128)(2,1)S(1)}, u32[]{:S(2)}, u32[]{:S(2)}) %collective-permute-start.1) | collective-permute-done | bytes 1179680 | tf_op jit(solution)/shard_map/ppermute | solution.py:34
  715.8 5.3 gather_fusion
  729.9 7.7 fusion.72
  738.3 6.5 add_convert_fusion.2
  749.2 8.5 fusion.71
  761.5 63.2 %reduce-scatter.5.cloned.1.call-done = f32[96,2304]{1,0:T(8,128)} async-done(((f32[768,2304]{1,0:T(8,128)}), f32[96,2304]{1,0:T(8,128)}) %reduce-scatter.5.cloned.1.call-update) | async-done | bytes 884752 | tf_op jit(solution)/shard_map/reduce_scatter | solution.py:254
  826.7 3.3 fusion.69
  830.0 13.3 %all-reduce.10 = (bf16[768]{0:T(1024)(128)(2,1)S(1)}, bf16[768]{0:T(1024)(128)(2,1)S(1)}) all-reduce(f32[768]{0:T(1024)S(1)} %get-tuple-element.264, f32[768]{0:T(1024)S(1)} %get-tuple-element.262), channel_id=2, replica_groups=mesh['dp'=8,'seq'=4] {'dp'}, use_global_device_ids=true, to_apply=%region_16.17.clone | all-reduce | flops 1536 | bytes 9216
  843.5 12.3 %all-reduce.12 = (bf16[96]{0:T(256)(128)(2,1)S(1)}, bf16[96]{0:T(256)(128)(2,1)S(1)}) all-reduce(bf16[96]{0:T(256)(128)(2,1)S(1)} %dynamic-slice.9, bf16[96]{0:T(256)(128)(2,1)S(1)} %dynamic-slice.8), channel_id=1, replica_groups=mesh['dp'=8,'seq'=4] {'seq'}, use_global_device_ids=true, to_apply=%region_17.18 | all-reduce | flops 192 | bytes 768 | tf_op jit(solution)/shard_map/psum | solution.py:266
  856.8 5.5 add_convert_fusion.1
  864.9 23.3 %all-reduce.16.cloned.1.call-done = (bf16[96,2304]{1,0:T(8,128)(2,1)}, bf16[96,768]{1,0:T(8,128)(2,1)}, bf16[96,2304]{1,0:T(8,128)(2,1)}, bf16[144,768]{1,0:T(8,128)(2,1)}) async-done(((bf16[96,2304]{1,0:T(8,128)(2,1)}, bf16[96,768]{1,0:T(8,128)(2,1)}, bf16[96,2304]{1,0:T(8,128)(2,1)}, bf16[144,768]{1,0:T(8,128)(2,1)}), (bf16[96,2304]{1,0:T(8,128)(2,1)}, bf16[96,768]{1,0:T(8,128)(2,1)}, ...) | async-done | bytes 1253392 | tf_op jit(solution)/shard_map/psum | solution.py:262
  (330 shorter events, 207.4 us)
Async XLA Ops:
  7.2 2.5 copy-start.28
  7.2 3.9 copy-start.29
  7.2 4.1 copy-start.30
  7.2 39.5 %all-gather.5.cloned.1.call-start = ((), (), s32[]{:S(2)}) async-start(), calls=%async_computation.7 | async-start | bytes 3981312 | tf_op jit(solution)/shard_map/all_gather | solution.py:160
  9.7 356.7 %copy-start.1 = (bf16[1024,768]{0,1:T(8,128)(2,1)}, bf16[1024,768]{0,1:T(8,128)(2,1)S(1)}, u32[]{:S(2)}) copy-start(bf16[1024,768]{0,1:T(8,128)(2,1)S(1)} %copy.56) | copy-start | bytes 4718596
  26.9 26.0 %copy-start.22 = (f32[768]{0:T(1024)}, f32[768]{0:T(1024)S(1)}, u32[]{:S(2)}) copy-start(f32[768]{0:T(1024)S(1)} %convert_element_type.142) | copy-start | bytes 9220
  28.2 38.7 %copy-start.12 = (f32[1024,64]{0,1:T(8,128)}, f32[1024,64]{0,1:T(8,128)S(1)}, u32[]{:S(2)}) copy-start(f32[1024,64]{0,1:T(8,128)S(1)} %get-tuple-element.350) | copy-start | bytes 786436
  28.5 24.4 %copy-start.20 = (f32[1024]{0:T(1024)}, f32[1024]{0:T(1024)S(1)}, u32[]{:S(2)}) copy-start(f32[1024]{0:T(1024)S(1)} %broadcast_multiply_fusion.1) | copy-start | bytes 12292
  29.0 23.9 %copy-start.26 = (f32[1024]{0:T(1024)}, f32[1024]{0:T(1024)S(1)}, u32[]{:S(2)}) copy-start(f32[1024]{0:T(1024)S(1)} %fusion.70) | copy-start | bytes 12292
  29.0 23.9 %copy-start.24 = (f32[1024]{0:T(1024)}, f32[1024]{0:T(1024)S(1)}, u32[]{:S(2)}) copy-start(f32[1024]{0:T(1024)S(1)} %fusion.83) | copy-start | bytes 12292
  63.3 4.0 slice-start
  63.3 4.7 slice-start.1
  63.3 4.7 copy-start.14
  91.8 144.2 %all-to-all-start = ((bf16[1024,3,768]{0,1,2:T(4,128)(2,1)}), bf16[1024,3,768]{0,1,2:T(4,128)(2,1)}, u32[]{:S(2)}, u32[]{:S(2)}) async-start(bf16[1024,3,768]{0,1,2:T(4,128)(2,1)} %copy.60), calls=%async_computation | async-start | bytes 12582912 | tf_op jit(solution)/shard_map/all_to_all | solution.py:188
  97.2 235.7 %all-gather.7.cloned.1.call-start = ((), (), s32[]{:S(2)}) async-start(), calls=%async_computation.8 | async-start | bytes 1327104 | tf_op jit(solution)/shard_map/all_gather | solution.py:161
  97.9 273.9 %all-gather.9.cloned.1.call-start = ((), (), s32[]{:S(2)}) async-start(), calls=%async_computation.9 | async-start | bytes 3981312 | tf_op jit(solution)/shard_map/all_gather | solution.py:162
  325.1 41.3 %all-to-all-start.1 = ((bf16[4,1024,192]{1,2,0:T(8,128)(2,1)}), bf16[4,1024,192]{1,2,0:T(8,128)(2,1)}, u32[]{:S(2)}, u32[]{:S(2)}) async-start(bf16[4,1024,192]{1,2,0:T(8,128)(2,1)} %copy.64), calls=%async_computation.1 | async-start | bytes 3145728 | tf_op jit(solution)/shard_map/all_to_all | solution.py:198
  329.5 53.0 %all-gather.11.cloned.1.call-start = ((), (), s32[]{:S(2)}) async-start(), calls=%async_computation.10 | async-start | bytes 1990656 | tf_op jit(solution)/shard_map/all_gather | solution.py:163
  330.1 417.5 %reduce-scatter.7.cloned.1.call-start = ((), (), s32[]{:S(2)}) async-start(), calls=%async_computation.12 | async-start | bytes 2654208 | tf_op jit(solution)/shard_map/reduce_scatter | solution.py:255
  369.7 1.7 copy-start.6
  371.8 10.7 %copy-start.16 = (bf16[1024,768]{1,0:T(8,128)(2,1)S(1)}, bf16[1024,768]{1,0:T(8,128)(2,1)}, u32[]{:S(2)}) copy-start(bf16[1024,768]{1,0:T(8,128)(2,1)} %param.19) | copy-start | bytes 4718596
  382.5 14.9 %copy-start.8 = (f32[1024,2304]{1,0:T(8,128)S(1)}, f32[1024,2304]{1,0:T(8,128)}, u32[]{:S(2)}) copy-start(f32[1024,2304]{1,0:T(8,128)} %fusion.91) | copy-start | bytes 28311556
  397.4 3.6 copy-start.7
  401.0 9.0 copy-start.10
  410.0 1.4 copy-start.4
  410.8 1.7 copy-start.3
  412.5 1.1 copy-start.17
  417.9 339.9 %reduce-scatter.11.cloned.1.call-start = ((), (), s32[]{:S(2)}) async-start(), calls=%async_computation.14 | async-start | bytes 3981312 | tf_op jit(solution)/shard_map/reduce_scatter | solution.py:257
  423.4 1.5 copy-start.18
  428.8 40.0 %all-to-all-start.2 = ((bf16[1024,4,192]{0,2,1:T(8,128)(2,1)}), bf16[1024,4,192]{0,2,1:T(8,128)(2,1)S(1)}, u32[]{:S(2)}, u32[]{:S(2)}) async-start(bf16[1024,4,192]{0,2,1:T(8,128)(2,1)} %bitcast.143), calls=%async_computation.2 | async-start | bytes 3145728 | tf_op jit(solution)/shard_map/all_to_all | solution.py:222
  432.4 327.2 %reduce-scatter.9.cloned.1.call-start = ((), (), s32[]{:S(2)}) async-start(), calls=%async_computation.13 | async-start | bytes 7962624 | tf_op jit(solution)/shard_map/reduce_scatter | solution.py:256
  444.0 380.8 %reduce-scatter.5.cloned.1.call-start = ((), (), s32[]{:S(2)}) async-start(), calls=%async_computation.11 | async-start | bytes 7962624 | tf_op jit(solution)/shard_map/reduce_scatter | solution.py:254
  485.5 4.0 copy-start
  502.2 4.1 copy-start
  518.9 4.6 copy-start
  536.3 4.4 copy-start
  553.2 4.0 copy-start
  569.9 4.0 copy-start
  586.6 4.0 copy-start
  603.2 4.0 copy-start
  631.1 1.4 copy-start.9
  633.5 30.9 %collective-permute-start = (bf16[1024,3,192]{0,2,1:T(8,128)(2,1)S(1)}, bf16[1024,3,192]{0,2,1:T(8,128)(2,1)S(1)}, u32[]{:S(2)}, u32[]{:S(2)}) collective-permute-start(bf16[1024,3,192]{0,2,1:T(8,128)(2,1)S(1)} %get-tuple-element.334), channel_id=1, source_target_pairs={{0,1},{1,2},{2,3},{3,0},{4,5},{5,6},{6,7},{7,4},{8,9},{9,10},{10,1... | collective-permute-start | bytes 3538952 | tf_op jit(solution)/shard_map/ppermute | solution.py:34
  633.5 79.6 %collective-permute-start.1 = (bf16[1024,3,192]{0,2,1:T(8,128)(2,1)S(1)}, bf16[1024,3,192]{0,2,1:T(8,128)(2,1)S(1)}, u32[]{:S(2)}, u32[]{:S(2)}) collective-permute-start(bf16[1024,3,192]{0,2,1:T(8,128)(2,1)S(1)} %get-tuple-element.333), channel_id=1, source_target_pairs={{0,2},{1,3},{2,0},{3,1},{4,6},{5,7},{6,4},{7,5},{8,10},{9,11},{10,... | collective-permute-start | bytes 3538952 | tf_op jit(solution)/shard_map/ppermute | solution.py:34
  635.9 77.2 %collective-permute-start.2 = (bf16[1024,3,192]{0,2,1:T(8,128)(2,1)S(1)}, bf16[1024,3,192]{0,2,1:T(8,128)(2,1)S(1)}, u32[]{:S(2)}, u32[]{:S(2)}) collective-permute-start(bf16[1024,3,192]{0,2,1:T(8,128)(2,1)S(1)} %get-tuple-element.332), channel_id=1, source_target_pairs={{0,3},{1,0},{2,1},{3,2},{4,7},{5,4},{6,5},{7,6},{8,11},{9,8},{10,9... | collective-permute-start | bytes 3538952 | tf_op jit(solution)/shard_map/ppermute | solution.py:34
  724.0 1.0 copy-start.15
  725.8 1.0 copy-start.13
  726.8 3.1 copy-start.2
  726.8 3.1 copy-start.21
  726.8 3.1 copy-start.23
  726.8 3.1 copy-start.25
  728.2 1.7 copy-start.11
  737.6 150.6 %all-reduce.16.cloned.1.call-start = ((), (), s32[]{:S(2)}) async-start(), calls=%async_computation.15 | async-start | bytes 2506752 | tf_op jit(solution)/shard_map/psum | solution.py:262
  749.2 8.5 copy-start.27
  826.7 30.1 %copy-start.5 = (bf16[1024,768]{0,1:T(8,128)(2,1)S(1)}, bf16[1024,768]{0,1:T(8,128)(2,1)}, u32[]{:S(2)}) copy-start(bf16[1024,768]{0,1:T(8,128)(2,1)} %copy.66) | copy-start | bytes 4718596
  888.2 5.7 copy-start.19
Sparse Core Ops, SparseCore 0:
  9.9 36.7 all-gather.4
  99.9 24.4 all-gather.6
  126.3 33.9 all-gather.8
  331.9 26.9 all-gather.10
  418.0 40.6 reduce-scatter.6
  462.4 48.0 reduce-scatter.10
  514.5 65.4 reduce-scatter.8
  737.7 86.9 reduce-scatter.4
  828.2 59.9 all-reduce.15
